TPU v7x, 32 devices: a whole 2x2x4 slice. The times are simulated.
32 devices in a mesh: groups: 2 (over x), dp: 16 (over z, y, core).
Axes of the slice: x: 2, y: 2, z: 4, core: 2. Of those that a mesh axis runs over, the one named last changes fastest.
Arguments:
- activations: bfloat16 [128, 176, 4096], P(('groups', 'dp')), parts along dimension 0, may hold values from -6 to 6
- cotangent: bfloat16 [128, 176, 1024], P(('groups', 'dp')), parts along dimension 0, may hold values from -6 to 6
- lengths: int32 [128], P(('groups', 'dp')), parts along dimension 0, may hold values from 44 to 176, as said below
- handover: int32 [128], P(('groups', 'dp')), parts along dimension 0, may hold values from 0 to 1, as said below
- adapter_down_factor: bfloat16 [64, 4096], replicated, may hold values from -0.09375 to 0.09375
- adapter_up_factor: bfloat16 [1024, 64], replicated, may hold values from -0.75 to 0.75
- output_feature_projection: bfloat16 [1024, 64], replicated, as said below
- up_rank_projection: bfloat16 [64, 64], replicated, as said below
- input_feature_projection: bfloat16 [4096, 64], replicated, as said below
- down_rank_projection: bfloat16 [64, 64], replicated, as said below
Outputs:
- feature_store: float32 [192, 8192], P(('groups', 'dp')), parts along dimension 0
- gram_panel: float32 [16384, 8192], P(('groups', 'dp')), parts along dimension 0
There are 2 independent parts, one for each index of `groups`. A program takes and returns all parts, laid end to end along the dimension named above; an argument that names none is the same for every part. Nothing has to cross between parts.
Inputs may be any that keep to these rules, and one draw needn't show every extreme that they name: `lengths`: some example has exactly 176 live tokens. At most 2 of the 4 examples of one index of dp have handover 1, and some index has exactly 2. `output_feature_projection`: every entry is plus or minus one over the square root of the number of rows. `up_rank_projection`: every entry is plus or minus one over the square root of the number of rows. `input_feature_projection`: every entry is plus or minus one over the square root of the number of rows. `down_rank_projection`: every entry is plus or minus one over the square root of the number of rows.
All inputs are finite; a program needn't handle non-finite values.
Results may differ from a plain program's by a relative error of at most 0.007.
Values may be sent and summed in bfloat16 or wider, within the bound.
A program may use at most 128 MiB of HBM per device.

v0:
```python
import math

import jax
import jax.numpy as jnp
from jax import lax
from jax.sharding import PartitionSpec as P

MOVED = 2


def from_behind(block, axis, distance):
    devices = range(lax.axis_size(axis))
    route = [((i - distance) % len(devices), i) for i in devices]
    return lax.ppermute(block, axis, route)


def per_token_features(
    activations,
    cotangent,
    lengths,
    adapter_down_factor,
    adapter_up_factor,
    output_feature_projection,
    up_rank_projection,
    input_feature_projection,
    down_rank_projection,
):
    examples, span, width = activations.shape
    projected_rank_width = adapter_down_factor.shape[0]
    side = input_feature_projection.shape[1]
    input_projection_matrix = jnp.concatenate(
        [adapter_down_factor.T, input_feature_projection], axis=1
    )
    output_projection_matrix = jnp.concatenate(
        [adapter_up_factor, output_feature_projection], axis=1
    )
    input_side = jnp.dot(
        activations.reshape(examples * span, width),
        input_projection_matrix,
        preferred_element_type=jnp.float32,
    ).astype(jnp.bfloat16)
    output_side = jnp.dot(
        cotangent.reshape(examples * span, cotangent.shape[2]),
        output_projection_matrix,
        preferred_element_type=jnp.float32,
    ).astype(jnp.bfloat16)
    reduced_down_gradient = input_side[:, :projected_rank_width]
    in_side = input_side[:, projected_rank_width:]
    reduced_up_gradient = output_side[:, :projected_rank_width]
    out_side = output_side[:, projected_rank_width:]
    rank_b = jnp.dot(
        reduced_down_gradient, up_rank_projection, preferred_element_type=jnp.float32
    ).astype(jnp.bfloat16)
    rank_a = jnp.dot(
        reduced_up_gradient, down_rank_projection, preferred_element_type=jnp.float32
    ).astype(jnp.bfloat16)
    live = (jnp.arange(span, dtype=jnp.int32)[None, :] < lengths[:, None]).reshape(
        examples * span, 1
    )
    out_live = jnp.where(live, out_side, jnp.zeros_like(out_side)).reshape(examples, span, side)
    rank_a_live = jnp.where(live, rank_a, jnp.zeros_like(rank_a)).reshape(examples, span, side)
    grad_b = jnp.einsum(
        "nti,ntj->nij",
        out_live,
        rank_b.reshape(examples, span, side),
        preferred_element_type=jnp.float32,
    )
    grad_a = jnp.einsum(
        "nti,ntj->nij",
        rank_a_live,
        in_side.reshape(examples, span, side),
        preferred_element_type=jnp.float32,
    )
    inv_root = lax.rsqrt(jnp.maximum(lengths, 1).astype(jnp.float32))
    stacked = jnp.concatenate(
        [grad_b.reshape(examples, side * side), grad_a.reshape(examples, side * side)], axis=1
    )
    return stacked * inv_root[:, None]


def shards(
    activations,
    cotangent,
    lengths,
    handover,
    adapter_down_factor,
    adapter_up_factor,
    output_feature_projection,
    up_rank_projection,
    input_feature_projection,
    down_rank_projection,
):
    examples = activations.shape[0]
    projection_weights = (
        adapter_down_factor,
        adapter_up_factor,
        output_feature_projection,
        up_rank_projection,
        input_feature_projection,
        down_rank_projection,
    )
    kept_share = (1 - handover).astype(jnp.float32)
    earlier = jnp.cumsum(handover) - handover
    slot_ids = jnp.arange(MOVED, dtype=jnp.int32)
    chooser = (handover[None, :] == 1) & (earlier[None, :] == slot_ids[:, None])
    feature_width = 2 * input_feature_projection.shape[1] * input_feature_projection.shape[1]
    panel_width = feature_width // lax.axis_size("dp")
    panel_start = lax.axis_index("dp") * panel_width
    total_examples = examples * lax.axis_size("dp")
    example_features = per_token_features(activations, cotangent, lengths, *projection_weights)
    packed = jnp.dot(
        chooser.astype(jnp.float32),
        example_features,
        precision=lax.Precision.HIGHEST,
        preferred_element_type=jnp.float32,
    )
    incoming = from_behind(packed, "dp", 1)
    feature_store = jnp.concatenate([example_features * kept_share[:, None], incoming], axis=0)
    shard_rows = lax.all_gather(feature_store, "dp", axis=0, tiled=True)
    panel_cols = lax.dynamic_slice_in_dim(shard_rows, panel_start, panel_width, 1)
    gram_panel = lax.dot_general(
        panel_cols,
        shard_rows,
        (((0,), (0,)), ((), ())),
        precision=lax.Precision.HIGHEST,
        preferred_element_type=jnp.float32,
    )
    gram_panel = gram_panel * (1.0 / math.sqrt(total_examples))
    return (feature_store, gram_panel)


def solution(mesh):
    in_specs = (
        P(("groups", "dp"), None, None),
        P(("groups", "dp"), None, None),
        P(("groups", "dp")),
        P(("groups", "dp")),
        P(),
        P(),
        P(),
        P(),
        P(),
        P(),
    )
    out_specs = (P(("groups", "dp"), None), P(("groups", "dp"), None))
    return jax.shard_map(shards, mesh=mesh, in_specs=in_specs, out_specs=out_specs, check_vma=False)
```

profile of v0, /device:TPU:0, one launch (start us, length us, event | category | flops | bytes accessed | tf_op | source)
XLA Modules:
  0.0 101.9 jit_solution(3518848702388114315)
XLA Ops:
  7.2 0.0 copy-start
  7.2 0.0 all-gather.3.cloned.1.call-start
  7.2 0.8 iota_compare_fusion
  8.1 0.7 convert_rsqrt_fusion
  8.7 0.1 lt.26
  8.8 0.0 copy-start.3
  8.8 0.0 copy-start.1
  8.8 0.0 copy-start.2
  8.8 4.7 %fusion.1 = bf16[704,128]{1,0:T(8,128)(2,1)S(1)} fusion(bf16[704,4096]{1,0:T(8,128)(2,1)} %bitcast.30, bf16[4096,64]{0,1:T(8,128)(2,1)} %param.18, bf16[4096,64]{0,1:T(8,128)(2,1)} %bitcast.31), kind=kOutput, calls=%fused_computation.5 | convolution fusion | flops 740384768 | bytes 6995968 | tf_op jit(solution)/shard_map/dot_general | solution.py:37
  13.5 0.0 copy-start.5
  13.5 0.0 copy-start.4
  13.5 0.1 slice.19
  13.7 0.0 copy-done.3
  13.7 0.2 convolution_convert_fusion.3
  13.9 0.1 reshape.78
  14.1 0.0 copy-done
  14.1 0.0 copy-done.1
  14.1 0.0 copy-done.2
  14.1 0.6 fusion.2
  14.6 0.2 slice_select_fusion
  14.9 0.2 fusion.12
  15.1 0.1 reshape.79
  15.2 0.0 copy-done.5
  15.2 0.2 fusion
  15.4 0.2 fusion.26
  15.6 0.1 reshape.82
  15.8 0.0 copy-done.4
  15.8 0.2 reduce-window.9
  16.0 0.3 fusion.14
  16.3 0.5 collective-permute-start
  16.8 0.1 fusion.15
  16.9 6.8 %collective-permute-done = f32[2,8192]{1,0:T(2,128)S(1)} collective-permute-done((f32[2,8192]{1,0:T(2,128)S(1)}, f32[2,8192]{1,0:T(2,128)S(1)}, u32[]{:S(2)}, u32[]{:S(2)}) %collective-permute-start) | collective-permute-done | bytes 65568 | tf_op jit(solution)/shard_map/ppermute | solution.py:14
  23.8 0.8 fusion.35
  24.5 0.0 all-gather.3.cloned.1.call-update
  24.5 0.8 pad_maximum_fusion
  25.3 48.9 %all-gather.3.cloned.1.call-done = f32[16,6,8192]{2,1,0:T(8,128)} async-done(((f32[1,6,8192]{2,1,0:T(8,128)}), f32[16,6,8192]{2,1,0:T(8,128)}) %all-gather.3.cloned.1.call-update) | async-done | bytes 3145744 | tf_op jit(solution)/shard_map/all_gather | solution.py:119
  74.2 3.6 %reshape.86 = f32[96,8192]{1,0:T(8,128)} reshape(f32[16,6,8192]{2,1,0:T(8,128)} %all-gather.3.cloned.1.call-done) | data formatting | bytes 6291456
  77.9 17.1 %convolution_multiply_fusion = f32[512,8192]{1,0:T(8,128)} fusion(f32[96,8192]{1,0:T(8,128)} %reshape.86, s32[]{:T(128)S(6)} %select_n.12), kind=kOutput, calls=%fused_computation | convolution fusion | flops 4836032512 | bytes 20119556 | tf_op jit(solution)/shard_map/dot_general | solution.py:121
  (2 shorter events, 0.0 us)
Async XLA Ops:
  7.2 6.9 %copy-start = (bf16[4,176,1024]{2,1,0:T(8,128)(2,1)S(1)}, bf16[4,176,1024]{2,1,0:T(8,128)(2,1)}, u32[]{:S(2)}) copy-start(bf16[4,176,1024]{2,1,0:T(8,128)(2,1)} %param.11) | copy-start | bytes 4325380
  7.2 67.1 %all-gather.3.cloned.1.call-start = ((), (), s32[]{:S(2)}) async-start(), calls=%async_computation | async-start | bytes 4456448 | tf_op jit(solution)/shard_map/all_gather | solution.py:119
  8.8 4.9 %copy-start.3 = (bf16[64,64]{1,0:T(8,128)(2,1)S(1)}, bf16[64,64]{1,0:T(8,128)(2,1)}, u32[]{:S(2)}) copy-start(bf16[64,64]{1,0:T(8,128)(2,1)} %param.17) | copy-start | bytes 24580
  8.8 5.3 %copy-start.1 = (bf16[1024,64]{0,1:T(8,128)(2,1)S(1)}, bf16[1024,64]{0,1:T(8,128)(2,1)}, u32[]{:S(2)}) copy-start(bf16[1024,64]{0,1:T(8,128)(2,1)} %param.16) | copy-start | bytes 393220
  8.8 5.3 %copy-start.2 = (bf16[1024,64]{0,1:T(8,128)(2,1)S(1)}, bf16[1024,64]{0,1:T(8,128)(2,1)}, u32[]{:S(2)}) copy-start(bf16[1024,64]{0,1:T(8,128)(2,1)} %param.15) | copy-start | bytes 393220
  13.5 1.7 %copy-start.5 = (bf16[64,64]{1,0:T(8,128)(2,1)S(1)}, bf16[64,64]{1,0:T(8,128)(2,1)}, u32[]{:S(2)}) copy-start(bf16[64,64]{1,0:T(8,128)(2,1)} %param.19) | copy-start | bytes 24580
  13.5 2.2 %copy-start.4 = (s32[4]{0:T(128)S(1)}, s32[4]{0:T(128)}, u32[]{:S(2)}) copy-start(s32[4]{0:T(128)} %param.13) | copy-start | bytes 52
  16.3 7.5 %collective-permute-start = (f32[2,8192]{1,0:T(2,128)S(1)}, f32[2,8192]{1,0:T(2,128)S(1)}, u32[]{:S(2)}, u32[]{:S(2)}) collective-permute-start(f32[2,8192]{1,0:T(2,128)S(1)} %fusion.14), channel_id=1, source_target_pairs={{15,0},{0,1},{1,2},{2,3},{3,4},{4,5},{5,6},{6,7},{7,8},{8,9},{9,10... | collective-permute-start | bytes 196616 | tf_op jit(solution)/shard_map/ppermute | solution.py:14
Sparse Core Ops, SparseCore 0:
  24.7 49.5 all-gather.2
where the time goes:
time: 102 us
  waiting for transfers between devices  55.8 us (55%)
  matrix products  23.6 us (23%)
  between operations  14.2 us (14%)
  local copies, waits for them, and re-layouts  4.25 us (4%)
  other arithmetic  3.5 us (3%)
    all_gather x1, waiting for transfers between devices, shards(): shard_rows = lax.all_gather(feature_store, 'dp', axis=0, tiled=True)  48.9 us
    dot_general x1, matrix products, shards(): lax.dot_general(panel_cols, shard_rows, (((0,), (0,)), ((), ())), precisi...  17.1 us
    ppermute x1, waiting for transfers between devices, from_behind(): return lax.ppermute(block, axis, route)  6.84 us
    dot_general x1, matrix products, per_token_features(): jnp.dot(activations.reshape(examples * span, width), input_projection_mat...  4.67 us
    unnamed x13, local copies, waits for them, and re-layouts  3.67 us
  transfers between devices with their start and end apart: 2, of which 2 were waited for; matrix products, arithmetic and copies ran while one was open for 1% of the time, Pallas kernels for 0%

commit v1 on v0

v1 whole, which is shorter than its diff:
```python
import functools
import math

import jax
import jax.numpy as jnp
from jax import lax
from jax.experimental import pallas as pl
from jax.experimental.pallas import tpu as pltpu
from jax.sharding import PartitionSpec as P

MOVED = 2
LANES = 128
DEPTH_CHUNKS = 8
COT_CHUNKS = 2
MESH = pl.DeviceIdType.MESH
F32 = jnp.float32
BF16 = jnp.bfloat16
NT = (((1,), (1,)), ((), ()))
TN = (((0,), (0,)), ((), ()))


def features_kernel(
    n, lengths_ref, handover_ref, act_ref, cot_ref, down_ref, up_ref, outp_ref, upr_ref, inp_ref,
    downr_ref, full_ref, rows_ref, act, cot, w_in, w_out, w_b, w_a, acc, block, inter, packed,
    arrived, act_sem, cot_sem, w_sem, z_send, y_send, core_send, recv, next_send, next_recv,
):
    examples = lengths_ref.shape[0]
    tokens, width = act_ref.shape
    span = tokens // examples
    side = down_ref.shape[0]
    out_width = cot_ref.shape[1]
    me = lax.axis_index("dp")
    group = lax.axis_index("groups")
    lines = n // 4
    z, y, c = me // 4, (me // 2) % 2, me % 2

    def at(zz, yy, cc):
        return zz * 4 + yy * 2 + cc

    def flip(value, mask):
        bit = 1
        while bit <= mask:
            if mask & bit:
                value = value + bit - 2 * bit * ((value // bit) % 2)
            bit *= 2
        return value

    others = [flip(z, d) for d in range(1, lines)]
    core_mate, y_mate = at(z, y, 1 - c), at(z, 1 - y, c)
    after, before = lax.rem(me + 1, n), lax.rem(me + n - 1, n)

    barrier = pltpu.get_barrier_semaphore()
    mates = [core_mate, y_mate, after, before] + [at(o, y, c) for o in others]
    for mate in mates:
        pl.semaphore_signal(barrier, inc=1, device_id=(group, mate), device_id_type=MESH)

    w_copies = [
        pltpu.make_async_copy(outp_ref, w_out.at[:side], w_sem.at[0]),
        pltpu.make_async_copy(up_ref, w_out.at[side:], w_sem.at[1]),
        pltpu.make_async_copy(down_ref, w_in.at[:side], w_sem.at[2]),
        pltpu.make_async_copy(inp_ref, w_in.at[side:], w_sem.at[3]),
    ]
    cot_step = tokens // COT_CHUNKS
    cot_copies = [
        pltpu.make_async_copy(
            cot_ref.at[pl.ds(i * cot_step, cot_step)], cot.at[pl.ds(i * cot_step, cot_step)],
            cot_sem.at[i],
        )
        for i in range(COT_CHUNKS)
    ]
    step = width // DEPTH_CHUNKS
    act_copies = [
        pltpu.make_async_copy(
            act_ref.at[:, pl.ds(i * step, step)], act.at[:, pl.ds(i * step, step)], act_sem.at[i]
        )
        for i in range(DEPTH_CHUNKS)
    ]
    for copy in w_copies[:2] + cot_copies + w_copies[2:] + act_copies:
        copy.start()

    w_b[...] = jnp.zeros_like(w_b)
    w_a[...] = jnp.zeros_like(w_a)
    w_b[:side, :side] = upr_ref[...]
    w_a[side:, side:] = downr_ref[...]

    lane = lax.broadcasted_iota(jnp.int32, (cot_step, LANES), 1)
    w_copies[0].wait()
    w_copies[1].wait()
    left = []
    for i in range(COT_CHUNKS):
        cot_copies[i].wait()
        both = lax.dot_general(
            cot[pl.ds(i * cot_step, cot_step)], w_out[...], NT, preferred_element_type=F32
        ).astype(BF16)
        rank_a = jnp.dot(both, w_a[...], preferred_element_type=F32).astype(BF16)
        left.append(jnp.where(lane < side, both.astype(F32), rank_a.astype(F32)))

    w_copies[2].wait()
    w_copies[3].wait()
    for i in range(DEPTH_CHUNKS):
        act_copies[i].wait()
        cols = pl.ds(i * step, step)
        part = lax.dot_general(act[:, cols], w_in[:, cols], NT, preferred_element_type=F32)
        if i == 0:
            acc[...] = part
        else:
            acc[...] += part

    half_lane = lax.broadcasted_iota(jnp.int32, (side // 2, LANES), 1) < side
    span_lane = lax.broadcasted_iota(jnp.int32, (span, LANES), 1) < side
    span_row = lax.broadcasted_iota(jnp.int32, (span, LANES), 0)
    per_chunk = cot_step // span
    earlier = jnp.int32(0)
    moved = [None] * MOVED
    for e in range(examples):
        rows = pl.ds(e * span, span)
        both = acc[rows].astype(BF16)
        rank_b = jnp.dot(both, w_b[...], preferred_element_type=F32).astype(BF16)
        right = jnp.where(span_lane, rank_b.astype(F32), both.astype(F32)).astype(BF16)
        at_row = (e % per_chunk) * span
        mine = left[e // per_chunk][at_row : at_row + span]
        live = jnp.where(span_row < lengths_ref[e], mine, 0.0).astype(BF16)
        root = lax.rsqrt(jnp.full((1, LANES), jnp.maximum(lengths_ref[e], 1).astype(F32)))
        block[e] = lax.dot_general(live, right, TN, preferred_element_type=F32) * root
        even = block[e, pl.ds(0, side, stride=2), :]
        odd = block[e, pl.ds(1, side, stride=2), :]
        half = side // 2
        top = jnp.where(half_lane, even[:half], pltpu.roll(odd[:half], LANES // 2, 1))
        low = jnp.where(half_lane, pltpu.roll(even[half:], LANES // 2, 1), odd[half:])
        flat = jnp.concatenate([top, low], axis=0)
        inter[pl.ds(e, side, stride=examples), :] = flat
        hand = handover_ref[e]
        rows_ref[pl.ds(e, side, stride=8), :] = flat * (1 - hand).astype(F32)
        for m in range(MOVED):
            share = jnp.where((hand == 1) & (earlier == m), 1.0, 0.0).astype(F32)
            term = flat * share
            moved[m] = term if moved[m] is None else moved[m] + term
        earlier = earlier + hand
    for m in range(MOVED):
        packed[m * side : (m + 1) * side] = moved[m].astype(BF16)
    full_ref[me] = inter[...].astype(BF16).reshape(full_ref.shape[1:])

    pl.semaphore_wait(barrier, len(mates))

    def send(slot, sem, mate):
        return pltpu.make_async_remote_copy(
            src_ref=full_ref.at[slot], dst_ref=full_ref.at[slot], send_sem=sem,
            recv_sem=recv.at[slot], device_id=(group, mate), device_id_type=MESH,
        )

    def landed(slot):
        send(slot, core_send.at[0], core_mate).wait_recv()

    started = []

    def go(slot, sem, mate):
        copy = send(slot, sem, mate)
        copy.start()
        started.append(copy)

    go(me, y_send.at[0], y_mate)
    for d, o in enumerate(others):
        go(me, z_send.at[d], at(o, y, c))
    go(me, core_send.at[0], core_mate)
    hop = pltpu.make_async_remote_copy(
        src_ref=packed, dst_ref=arrived, send_sem=next_send, recv_sem=next_recv,
        device_id=(group, after), device_id_type=MESH,
    )
    hop.start()
    for d, o in enumerate(others):
        slot = at(o, y, c)
        landed(slot)
        go(slot, y_send.at[1 + d], y_mate)
        go(slot, core_send.at[1 + d], core_mate)
    for d, o in enumerate([z] + others):
        slot = at(o, 1 - y, c)
        landed(slot)
        go(slot, core_send.at[lines + d], core_mate)
    hop.wait_recv()
    for m in range(MOVED):
        rows_ref[pl.ds(examples + m, side, stride=8), :] = arrived[
            m * side : (m + 1) * side
        ].astype(F32)
    for row in range(examples + MOVED, 8):
        rows_ref[pl.ds(row, side, stride=8), :] = jnp.zeros((side, LANES), F32)
    for o in [z] + others:
        landed(at(o, y, 1 - c))
    for o in [z] + others:
        landed(at(o, 1 - y, 1 - c))
    hop.wait_send()
    for copy in started:
        copy.wait_send()


def gram_kernel(n, examples, scale, full_ref, rows_ref, store_ref, gram_ref, panel):
    me = lax.axis_index("dp")
    j = pl.program_id(0)
    blocks = gram_ref.shape[0] // LANES
    depth = n * 16
    per_tile = 16 // examples

    @pl.when(j == 0)
    def _():
        lane = lax.broadcasted_iota(jnp.int32, (LANES, LANES), 1)
        for t in range(blocks):
            block = me * blocks + t
            place = t % per_tile if blocks % per_tile == 0 else block % per_tile
            columns = full_ref[:, block // per_tile].reshape(depth, LANES).astype(F32)
            for q in range(depth // LANES):
                turned = columns[q * LANES : (q + 1) * LANES].T * scale
                for m in range(per_tile):
                    shift = (examples * (m - place) + LANES) % LANES
                    moved = turned
                    if not isinstance(shift, int) or shift:
                        moved = pltpu.roll(turned, shift, 1)
                    keep = (lane // examples) % per_tile == m
                    panel[m, t * LANES : (t + 1) * LANES, q * LANES : (q + 1) * LANES] = jnp.where(
                        keep, moved, 0.0
                    ).astype(BF16)
        height = store_ref.shape[0]
        for r in range(store_ref.shape[1] // LANES):
            store_ref[:, r * LANES : (r + 1) * LANES] = rows_ref[r * 8 : r * 8 + height, :]

    tiles = gram_ref.shape[1] // (LANES * per_tile)
    right = jnp.concatenate(
        [full_ref[:, j * tiles + t].reshape(depth, LANES) for t in range(tiles)], axis=1
    )
    for m in range(per_tile):
        product = jnp.dot(panel[m], right, preferred_element_type=F32)
        for t in range(tiles):
            column = (t * per_tile + m) * LANES
            gram_ref[:, column : column + LANES] = product[:, t * LANES : (t + 1) * LANES]


def shards(
    activations,
    cotangent,
    lengths,
    handover,
    adapter_down_factor,
    adapter_up_factor,
    output_feature_projection,
    up_rank_projection,
    input_feature_projection,
    down_rank_projection,
):
    n = lax.axis_size("dp")
    examples, span, width = activations.shape
    out_width = cotangent.shape[2]
    side = input_feature_projection.shape[1]
    tokens = examples * span
    feature_width = 2 * side * side
    tiles = feature_width // LANES * examples // 16
    dma = pltpu.SemaphoreType.DMA
    vmem = pl.BlockSpec(memory_space=pltpu.VMEM)
    smem = pl.BlockSpec(memory_space=pltpu.SMEM)
    far = pl.BlockSpec(memory_space=pl.ANY)
    full, rows = pl.pallas_call(
        functools.partial(features_kernel, n),
        out_shape=(
            jax.ShapeDtypeStruct((n, tiles, 16, LANES), BF16),
            jax.ShapeDtypeStruct((feature_width // LANES * 8, LANES), F32),
        ),
        in_specs=[smem, smem, far, far, far, far, far, vmem, far, vmem],
        out_specs=(vmem, vmem),
        scratch_shapes=[
            pltpu.VMEM((tokens, width), BF16),
            pltpu.VMEM((tokens, out_width), BF16),
            pltpu.VMEM((2 * side, width), BF16),
            pltpu.VMEM((2 * side, out_width), BF16),
            pltpu.VMEM((2 * side, 2 * side), BF16),
            pltpu.VMEM((2 * side, 2 * side), BF16),
            pltpu.VMEM((tokens, LANES), F32),
            pltpu.VMEM((examples, 2 * side, LANES), F32),
            pltpu.VMEM((examples * side, LANES), F32),
            pltpu.VMEM((MOVED * side, LANES), BF16),
            pltpu.VMEM((MOVED * side, LANES), BF16),
            dma((DEPTH_CHUNKS,)),
            dma((COT_CHUNKS,)),
            dma((4,)),
            dma((n // 4,)),
            dma((n // 4,)),
            dma((n // 2,)),
            dma((n,)),
            dma,
            dma,
        ],
        compiler_params=pltpu.CompilerParams(
            collective_id=0, has_side_effects=True, vmem_limit_bytes=48 * 2**20
        ),
        name="features",
    )(
        lengths,
        handover,
        activations.reshape(tokens, width),
        cotangent.reshape(tokens, out_width),
        adapter_down_factor,
        adapter_up_factor.T,
        output_feature_projection.T,
        up_rank_projection,
        input_feature_projection.T,
        down_rank_projection,
    )
    panel_width = feature_width // n
    grid = 8
    scale = 1.0 / math.sqrt(examples * n)
    return pl.pallas_call(
        functools.partial(gram_kernel, n, examples, scale),
        out_shape=(
            jax.ShapeDtypeStruct((examples + MOVED, feature_width), F32),
            jax.ShapeDtypeStruct((panel_width, feature_width), F32),
        ),
        grid=(grid,),
        in_specs=[vmem, vmem],
        out_specs=(
            pl.BlockSpec((examples + MOVED, feature_width), lambda j: (0, 0)),
            pl.BlockSpec((panel_width, feature_width // grid), lambda j: (0, j)),
        ),
        scratch_shapes=[pltpu.VMEM((16 // examples, panel_width, n * 16), BF16)],
        compiler_params=pltpu.CompilerParams(vmem_limit_bytes=32 * 2**20),
        name="gram",
    )(full, rows)


def solution(mesh):
    in_specs = (
        P(("groups", "dp"), None, None),
        P(("groups", "dp"), None, None),
        P(("groups", "dp")),
        P(("groups", "dp")),
        P(),
        P(),
        P(),
        P(),
        P(),
        P(),
    )
    out_specs = (P(("groups", "dp"), None), P(("groups", "dp"), None))
    return jax.shard_map(shards, mesh=mesh, in_specs=in_specs, out_specs=out_specs, check_vma=False)
```

time: 102 us -> 39.8 us (0.39)
  waiting for transfers between devices: 55.8 us -> 0 us
  Pallas kernels: 0 us -> 30.8 us
  matrix products: 23.6 us -> 0 us
  between operations: 14.2 us -> 0.66 us
  local copies, waits for them, and re-layouts: 4.25 us -> 7.99 us
  other arithmetic: 3.5 us -> 0 us
    all_gather x1 -> x0, waiting for transfers between devices: 48.9 us -> none  [shards(): shard_rows = lax.all_gather(feature_store, 'dp', axis=0, tiled=True)]
    pallas_call x0 -> x2, Pallas kernels: none -> 30.8 us  [the longest x1 22.5 us: shards(): pl.pallas_call(functools.partial(features_kernel, n), out_shape=(jax.Shap...]
    dot_general x8 -> x0, matrix products: 23.6 us -> none  [the longest x1 17.1 us: shards(): lax.dot_general(panel_cols, shard_rows, (((0,), (0,)), ((), ())), precisi...]
    ppermute x1 -> x0, waiting for transfers between devices: 6.84 us -> none  [from_behind(): return lax.ppermute(block, axis, route)]
    unnamed x13 -> x18, local copies, waits for them, and re-layouts: 3.67 us -> 7.99 us
  transfers between devices with their start and end apart: 2 -> 0, of which waited for: 2 -> 0; matrix products, arithmetic and copies ran while one was open for 1% -> 0% of each run, Pallas kernels for 0% -> 0%
where the time goes in v1:
time: 39.8 us; the launch traced here: 39.4 us
  Pallas kernels  30.8 us (77%)
  local copies, waits for them, and re-layouts  7.99 us (20%)
  between operations  0.66 us (2%)
    pallas_call x1, Pallas kernels, shards(): pl.pallas_call(functools.partial(features_kernel, n), out_shape=(jax.Shap...  22.5 us
    pallas_call x1, Pallas kernels, shards(): pl.pallas_call(functools.partial(gram_kernel, n, examples, scale), out_sh...  8.21 us
    unnamed x18, local copies, waits for them, and re-layouts  7.99 us

profile of v1, /device:TPU:0, one launch (start us, length us, event | category | flops | bytes accessed | tf_op | source)
XLA Modules:
  0.0 39.4 jit_solution(8578495302682478592)
XLA Ops:
  0.6 0.0 copy-start
  0.6 1.4 %copy-done = bf16[4,176,1024]{2,1,0:T(8,128)(2,1)S(1)} copy-done((bf16[4,176,1024]{2,1,0:T(8,128)(2,1)S(1)}, bf16[4,176,1024]{2,1,0:T(8,128)(2,1)}, u32[]{:S(2)}) %copy-start) | copy-done | bytes 1441816
  2.0 0.0 copy-start.1
  2.0 1.0 %copy-done.1 = bf16[64,4096]{1,0:T(8,128)(2,1)S(1)} copy-done((bf16[64,4096]{1,0:T(8,128)(2,1)S(1)}, bf16[64,4096]{1,0:T(8,128)(2,1)}, u32[]{:S(2)}) %copy-start.1) | copy-done | bytes 524312
  3.0 0.0 copy-start.2
  3.0 1.0 %copy-done.2 = bf16[4096,64]{0,1:T(8,128)(2,1)S(1)} copy-done((bf16[4096,64]{0,1:T(8,128)(2,1)S(1)}, bf16[4096,64]{0,1:T(8,128)(2,1)}, u32[]{:S(2)}) %copy-start.2) | copy-done | bytes 524312
  4.1 0.0 copy-start.3
  4.1 0.9 %copy-done.3 = bf16[1024,64]{0,1:T(8,128)(2,1)S(1)} copy-done((bf16[1024,64]{0,1:T(8,128)(2,1)S(1)}, bf16[1024,64]{0,1:T(8,128)(2,1)}, u32[]{:S(2)}) %copy-start.3) | copy-done | bytes 131096
  5.0 0.0 copy-start.4
  5.0 0.9 %copy-done.4 = bf16[1024,64]{0,1:T(8,128)(2,1)S(1)} copy-done((bf16[1024,64]{0,1:T(8,128)(2,1)S(1)}, bf16[1024,64]{0,1:T(8,128)(2,1)}, u32[]{:S(2)}) %copy-start.4) | copy-done | bytes 131096
  5.9 0.0 copy-start.5
  5.9 0.7 %copy-done.5 = bf16[64,64]{1,0:T(8,128)(2,1)S(1)} copy-done((bf16[64,64]{1,0:T(8,128)(2,1)S(1)}, bf16[64,64]{1,0:T(8,128)(2,1)}, u32[]{:S(2)}) %copy-start.5) | copy-done | bytes 8216
  6.6 0.0 copy-start.6
  6.6 0.7 %copy-done.6 = bf16[64,64]{1,0:T(8,128)(2,1)S(1)} copy-done((bf16[64,64]{1,0:T(8,128)(2,1)S(1)}, bf16[64,64]{1,0:T(8,128)(2,1)}, u32[]{:S(2)}) %copy-start.6) | copy-done | bytes 8216
  7.3 0.0 copy-start.7
  7.3 0.7 %copy-done.7 = s32[4]{0:T(128)S(1)} copy-done((s32[4]{0:T(128)S(1)}, s32[4]{0:T(128)}, u32[]{:S(2)}) %copy-start.7) | copy-done | bytes 40
  8.0 0.0 copy-start.8
  8.0 0.7 %copy-done.8 = s32[4]{0:T(128)S(1)} copy-done((s32[4]{0:T(128)S(1)}, s32[4]{0:T(128)}, u32[]{:S(2)}) %copy-start.8) | copy-done | bytes 40
  8.6 22.5 %features.1 = (bf16[16,16,16,128]{3,2,1,0:T(8,128)(2,1)S(1)}, f32[512,128]{1,0:T(8,128)S(1)}) custom-call(s32[4]{0:T(128)S(1)} %copy-done.7, s32[4]{0:T(128)S(1)} %copy-done.8, bf16[704,4096]{1,0:T(8,128)(2,1)} %bitcast.9, bf16[704,1024]{1,0:T(8,128)(2,1)S(1)} %bitcast.5, bf16[64,4096]{1,0:T(8,128)(2,1)S(1)} %copy-done.1, bf16[64,1024]{1,0:T(8,128)(2,1)S(1)} %bitcast.7, ...), custom_call_target="tpu_custom_call" | custom-call | tf_op jit(solution)/shard_map/features/pallas_call | solution.py:258
  31.2 8.2 %gram.1 = (f32[6,8192]{1,0:T(8,128)}, f32[512,8192]{1,0:T(8,128)}) custom-call(bf16[16,16,16,128]{3,2,1,0:T(8,128)(2,1)S(1)} %get-tuple-element.4.full_ref, f32[512,128]{1,0:T(8,128)S(1)} %get-tuple-element.5.rows_ref), custom_call_target="tpu_custom_call" | custom-call | tf_op jit(solution)/shard_map/gram/pallas_call | solution.py:307
Async XLA Ops:
  0.6 1.4 %copy-start = (bf16[4,176,1024]{2,1,0:T(8,128)(2,1)S(1)}, bf16[4,176,1024]{2,1,0:T(8,128)(2,1)}, u32[]{:S(2)}) copy-start(bf16[4,176,1024]{2,1,0:T(8,128)(2,1)} %param.11) | copy-start | bytes 4325380
  2.0 1.0 %copy-start.1 = (bf16[64,4096]{1,0:T(8,128)(2,1)S(1)}, bf16[64,4096]{1,0:T(8,128)(2,1)}, u32[]{:S(2)}) copy-start(bf16[64,4096]{1,0:T(8,128)(2,1)} %down_ref.1) | copy-start | bytes 1572868
  3.0 1.0 %copy-start.2 = (bf16[4096,64]{0,1:T(8,128)(2,1)S(1)}, bf16[4096,64]{0,1:T(8,128)(2,1)}, u32[]{:S(2)}) copy-start(bf16[4096,64]{0,1:T(8,128)(2,1)} %param.18) | copy-start | bytes 1572868
  4.1 0.9 %copy-start.3 = (bf16[1024,64]{0,1:T(8,128)(2,1)S(1)}, bf16[1024,64]{0,1:T(8,128)(2,1)}, u32[]{:S(2)}) copy-start(bf16[1024,64]{0,1:T(8,128)(2,1)} %param.15) | copy-start | bytes 393220
  5.0 0.9 %copy-start.4 = (bf16[1024,64]{0,1:T(8,128)(2,1)S(1)}, bf16[1024,64]{0,1:T(8,128)(2,1)}, u32[]{:S(2)}) copy-start(bf16[1024,64]{0,1:T(8,128)(2,1)} %param.16) | copy-start | bytes 393220
  5.9 0.7 %copy-start.5 = (bf16[64,64]{1,0:T(8,128)(2,1)S(1)}, bf16[64,64]{1,0:T(8,128)(2,1)}, u32[]{:S(2)}) copy-start(bf16[64,64]{1,0:T(8,128)(2,1)} %upr_ref.1) | copy-start | bytes 24580
  6.6 0.7 %copy-start.6 = (bf16[64,64]{1,0:T(8,128)(2,1)S(1)}, bf16[64,64]{1,0:T(8,128)(2,1)}, u32[]{:S(2)}) copy-start(bf16[64,64]{1,0:T(8,128)(2,1)} %downr_ref.1) | copy-start | bytes 24580
  7.3 0.7 %copy-start.7 = (s32[4]{0:T(128)S(1)}, s32[4]{0:T(128)}, u32[]{:S(2)}) copy-start(s32[4]{0:T(128)} %lengths_ref.1) | copy-start | bytes 52
  8.0 0.7 %copy-start.8 = (s32[4]{0:T(128)S(1)}, s32[4]{0:T(128)}, u32[]{:S(2)}) copy-start(s32[4]{0:T(128)} %handover_ref.1) | copy-start | bytes 52

commit v2 on v1

--- a/solution.py
+++ b/solution.py
@@ -20,11 +20,11 @@
 
 
 def features_kernel(
-    n, lengths_ref, handover_ref, act_ref, cot_ref, down_ref, up_ref, outp_ref, upr_ref, inp_ref,
-    downr_ref, full_ref, rows_ref, act, cot, w_in, w_out, w_b, w_a, acc, block, inter, packed,
-    arrived, act_sem, cot_sem, w_sem, z_send, y_send, core_send, recv, next_send, next_recv,
+    n, lengths_in, handover_in, act_ref, cot_ref, down_ref, up_ref, outp_ref, upr_in, inp_ref,
+    downr_in, full_ref, rows_out, mine_ref, rows_ref, lengths_ref, handover_ref, upr_ref, downr_ref, act, cot, w_in,
+    w_out, w_b, w_a, acc, block, inter, packed, arrived, out_sem, small_sem, act_sem, cot_sem, w_sem, z_send, y_send, core_send, recv, next_send, next_recv,
 ):
-    examples = lengths_ref.shape[0]
+    examples = lengths_in.shape[0]
     tokens, width = act_ref.shape
     span = tokens // examples
     side = down_ref.shape[0]
@@ -75,11 +75,24 @@
         )
         for i in range(DEPTH_CHUNKS)
     ]
-    for copy in w_copies[:2] + cot_copies + w_copies[2:] + act_copies:
+    small = [
+        pltpu.make_async_copy(source, target, small_sem.at[i])
+        for i, (source, target) in enumerate(
+            [
+                (upr_in, upr_ref),
+                (downr_in, downr_ref),
+                (lengths_in, lengths_ref),
+                (handover_in, handover_ref),
+            ]
+        )
+    ]
+    for copy in w_copies[:2] + small + cot_copies + w_copies[2:] + act_copies:
         copy.start()
 
     w_b[...] = jnp.zeros_like(w_b)
     w_a[...] = jnp.zeros_like(w_a)
+    for copy in small:
+        copy.wait()
     w_b[:side, :side] = upr_ref[...]
     w_a[side:, side:] = downr_ref[...]
 
@@ -138,13 +151,15 @@
         earlier = earlier + hand
     for m in range(MOVED):
         packed[m * side : (m + 1) * side] = moved[m].astype(BF16)
-    full_ref[me] = inter[...].astype(BF16).reshape(full_ref.shape[1:])
+    mine_ref[...] = inter[...].astype(BF16).reshape(mine_ref.shape)
+    keep = pltpu.make_async_copy(mine_ref, full_ref.at[me], out_sem.at[0])
+    keep.start()
 
     pl.semaphore_wait(barrier, len(mates))
 
-    def send(slot, sem, mate):
+    def send(slot, sem, mate, own=False):
         return pltpu.make_async_remote_copy(
-            src_ref=full_ref.at[slot], dst_ref=full_ref.at[slot], send_sem=sem,
+            src_ref=mine_ref if own else full_ref.at[slot], dst_ref=full_ref.at[slot], send_sem=sem,
             recv_sem=recv.at[slot], device_id=(group, mate), device_id_type=MESH,
         )
 
@@ -153,15 +168,15 @@
 
     started = []
 
-    def go(slot, sem, mate):
-        copy = send(slot, sem, mate)
+    def go(slot, sem, mate, own=False):
+        copy = send(slot, sem, mate, own)
         copy.start()
         started.append(copy)
 
-    go(me, y_send.at[0], y_mate)
+    go(me, y_send.at[0], y_mate, True)
     for d, o in enumerate(others):
-        go(me, z_send.at[d], at(o, y, c))
-    go(me, core_send.at[0], core_mate)
+        go(me, z_send.at[d], at(o, y, c), True)
+    go(me, core_send.at[0], core_mate, True)
     hop = pltpu.make_async_remote_copy(
         src_ref=packed, dst_ref=arrived, send_sem=next_send, recv_sem=next_recv,
         device_id=(group, after), device_id_type=MESH,
@@ -183,16 +198,22 @@
         ].astype(F32)
     for row in range(examples + MOVED, 8):
         rows_ref[pl.ds(row, side, stride=8), :] = jnp.zeros((side, LANES), F32)
+    keep_rows = pltpu.make_async_copy(rows_ref, rows_out, out_sem.at[1])
+    keep_rows.start()
     for o in [z] + others:
         landed(at(o, y, 1 - c))
     for o in [z] + others:
         landed(at(o, 1 - y, 1 - c))
     hop.wait_send()
+    keep.wait()
+    keep_rows.wait()
     for copy in started:
         copy.wait_send()
 
 
-def gram_kernel(n, examples, scale, full_ref, rows_ref, store_ref, gram_ref, panel):
+def gram_kernel(
+    n, examples, scale, full_in, rows_in, store_ref, gram_ref, panel, full_ref, rows_ref, sem
+):
     me = lax.axis_index("dp")
     j = pl.program_id(0)
     blocks = gram_ref.shape[0] // LANES
@@ -201,6 +222,10 @@
 
     @pl.when(j == 0)
     def _():
+        fetch = pltpu.make_async_copy(full_in, full_ref, sem.at[0])
+        fetch.start()
+        pltpu.make_async_copy(rows_in, rows_ref, sem.at[1]).start()
+        fetch.wait()
         lane = lax.broadcasted_iota(jnp.int32, (LANES, LANES), 1)
         for t in range(blocks):
             block = me * blocks + t
@@ -217,6 +242,10 @@
                     panel[m, t * LANES : (t + 1) * LANES, q * LANES : (q + 1) * LANES] = jnp.where(
                         keep, moved, 0.0
                     ).astype(BF16)
+
+    @pl.when(j == 1)
+    def _():
+        pltpu.make_async_copy(rows_in, rows_ref, sem.at[1]).wait()
         height = store_ref.shape[0]
         for r in range(store_ref.shape[1] // LANES):
             store_ref[:, r * LANES : (r + 1) * LANES] = rows_ref[r * 8 : r * 8 + height, :]
@@ -252,8 +281,6 @@
     feature_width = 2 * side * side
     tiles = feature_width // LANES * examples // 16
     dma = pltpu.SemaphoreType.DMA
-    vmem = pl.BlockSpec(memory_space=pltpu.VMEM)
-    smem = pl.BlockSpec(memory_space=pltpu.SMEM)
     far = pl.BlockSpec(memory_space=pl.ANY)
     full, rows = pl.pallas_call(
         functools.partial(features_kernel, n),
@@ -261,9 +288,15 @@
             jax.ShapeDtypeStruct((n, tiles, 16, LANES), BF16),
             jax.ShapeDtypeStruct((feature_width // LANES * 8, LANES), F32),
         ),
-        in_specs=[smem, smem, far, far, far, far, far, vmem, far, vmem],
-        out_specs=(vmem, vmem),
+        in_specs=[far] * 10,
+        out_specs=(far, far),
         scratch_shapes=[
+            pltpu.VMEM((tiles, 16, LANES), BF16),
+            pltpu.VMEM((feature_width // LANES * 8, LANES), F32),
+            pltpu.SMEM((examples,), jnp.int32),
+            pltpu.SMEM((examples,), jnp.int32),
+            pltpu.VMEM((side, side), BF16),
+            pltpu.VMEM((side, side), BF16),
             pltpu.VMEM((tokens, width), BF16),
             pltpu.VMEM((tokens, out_width), BF16),
             pltpu.VMEM((2 * side, width), BF16),
@@ -275,6 +308,8 @@
             pltpu.VMEM((examples * side, LANES), F32),
             pltpu.VMEM((MOVED * side, LANES), BF16),
             pltpu.VMEM((MOVED * side, LANES), BF16),
+            dma((2,)),
+            dma((4,)),
             dma((DEPTH_CHUNKS,)),
             dma((COT_CHUNKS,)),
             dma((4,)),
@@ -286,7 +321,7 @@
             dma,
         ],
         compiler_params=pltpu.CompilerParams(
-            collective_id=0, has_side_effects=True, vmem_limit_bytes=48 * 2**20
+            collective_id=0, has_side_effects=True, vmem_limit_bytes=60 * 2**20
         ),
         name="features",
     )(
@@ -311,13 +346,18 @@
             jax.ShapeDtypeStruct((panel_width, feature_width), F32),
         ),
         grid=(grid,),
-        in_specs=[vmem, vmem],
+        in_specs=[far, far],
         out_specs=(
             pl.BlockSpec((examples + MOVED, feature_width), lambda j: (0, 0)),
             pl.BlockSpec((panel_width, feature_width // grid), lambda j: (0, j)),
         ),
-        scratch_shapes=[pltpu.VMEM((16 // examples, panel_width, n * 16), BF16)],
-        compiler_params=pltpu.CompilerParams(vmem_limit_bytes=32 * 2**20),
+        scratch_shapes=[
+            pltpu.VMEM((16 // examples, panel_width, n * 16), BF16),
+            pltpu.VMEM(full.shape, BF16),
+            pltpu.VMEM(rows.shape, F32),
+            dma((2,)),
+        ],
+        compiler_params=pltpu.CompilerParams(vmem_limit_bytes=60 * 2**20),
         name="gram",
     )(full, rows)
 

time: 39.8 us -> 34.5 us (0.87)
  local copies, waits for them, and re-layouts: 7.99 us -> 0 us
  Pallas kernels: 30.8 us -> 33.7 us
    unnamed x18 -> x0, local copies, waits for them, and re-layouts: 7.99 us -> none
    pallas_call x1, Pallas kernels: 22.5 us -> 24.3 us  [shards(): pl.pallas_call(functools.partial(features_kernel, n), out_shape=(jax.Shap...]
    pallas_call x1, Pallas kernels: 8.21 us -> 9.4 us  [shards(): pl.pallas_call(functools.partial(gram_kernel, n, examples, scale), out_sh...]
where the time goes in v2:
time: 34.5 us; the launch traced here: 34.4 us
  Pallas kernels  33.7 us (98%)
  between operations  0.64 us (2%)
    pallas_call x1, Pallas kernels, shards(): pl.pallas_call(functools.partial(features_kernel, n), out_shape=(jax.Shap...  24.3 us
    pallas_call x1, Pallas kernels, shards(): pl.pallas_call(functools.partial(gram_kernel, n, examples, scale), out_sh...  9.4 us

profile of v2, /device:TPU:0, one launch (start us, length us, event | category | flops | bytes accessed | tf_op | source)
XLA Modules:
  0.0 34.4 jit_solution(17519612317143275651)
XLA Ops:
  0.6 24.3 %features.1 = (bf16[16,16,16,128]{3,2,1,0:T(8,128)(2,1)}, f32[512,128]{1,0:T(8,128)}) custom-call(s32[4]{0:T(128)} %lengths_in.1, s32[4]{0:T(128)} %handover_in.1, bf16[704,4096]{1,0:T(8,128)(2,1)} %bitcast.5, bf16[704,1024]{1,0:T(8,128)(2,1)} %bitcast.6, bf16[64,4096]{1,0:T(8,128)(2,1)} %down_ref.1, bf16[64,1024]{1,0:T(8,128)(2,1)} %bitcast.8, ...), custom_call_target="tpu_custom_call" | custom-call | tf_op jit(solution)/shard_map/features/pallas_call | solution.py:285
  25.0 9.4 %gram.1 = (f32[6,8192]{1,0:T(8,128)}, f32[512,8192]{1,0:T(8,128)}) custom-call(bf16[16,16,16,128]{3,2,1,0:T(8,128)(2,1)} %get-tuple-element.4.full_in, f32[512,128]{1,0:T(8,128)} %get-tuple-element.5.rows_in), custom_call_target="tpu_custom_call" | custom-call | tf_op jit(solution)/shard_map/gram/pallas_call | solution.py:342

commit v3 on v2

--- a/solution.py
+++ b/solution.py
@@ -10,7 +10,7 @@
 
 MOVED = 2
 LANES = 128
-DEPTH_CHUNKS = 8
+DEPTH_CHUNKS = 4
 COT_CHUNKS = 2
 MESH = pl.DeviceIdType.MESH
 F32 = jnp.float32
@@ -108,6 +108,14 @@
         rank_a = jnp.dot(both, w_a[...], preferred_element_type=F32).astype(BF16)
         left.append(jnp.where(lane < side, both.astype(F32), rank_a.astype(F32)))
 
+    span_row = lax.broadcasted_iota(jnp.int32, (span, LANES), 0)
+    per_chunk = cot_step // span
+    lives = []
+    for e in range(examples):
+        at_row = (e % per_chunk) * span
+        mine = left[e // per_chunk][at_row : at_row + span]
+        lives.append(jnp.where(span_row < lengths_ref[e], mine, 0.0).astype(BF16))
+
     w_copies[2].wait()
     w_copies[3].wait()
     for i in range(DEPTH_CHUNKS):
@@ -120,21 +128,21 @@
             acc[...] += part
 
     half_lane = lax.broadcasted_iota(jnp.int32, (side // 2, LANES), 1) < side
-    span_lane = lax.broadcasted_iota(jnp.int32, (span, LANES), 1) < side
-    span_row = lax.broadcasted_iota(jnp.int32, (span, LANES), 0)
-    per_chunk = cot_step // span
     earlier = jnp.int32(0)
     moved = [None] * MOVED
+    whole = acc[...].astype(BF16)
+    rank_b = jnp.dot(whole, w_b[...], preferred_element_type=F32).astype(BF16)
+    all_lane = lax.broadcasted_iota(jnp.int32, (tokens, LANES), 1) < side
+    right = jnp.where(all_lane, rank_b.astype(F32), whole.astype(F32)).astype(BF16)
     for e in range(examples):
-        rows = pl.ds(e * span, span)
-        both = acc[rows].astype(BF16)
-        rank_b = jnp.dot(both, w_b[...], preferred_element_type=F32).astype(BF16)
-        right = jnp.where(span_lane, rank_b.astype(F32), both.astype(F32)).astype(BF16)
-        at_row = (e % per_chunk) * span
-        mine = left[e // per_chunk][at_row : at_row + span]
-        live = jnp.where(span_row < lengths_ref[e], mine, 0.0).astype(BF16)
         root = lax.rsqrt(jnp.full((1, LANES), jnp.maximum(lengths_ref[e], 1).astype(F32)))
-        block[e] = lax.dot_general(live, right, TN, preferred_element_type=F32) * root
+        block[e] = (
+            lax.dot_general(
+                lives[e], right[e * span : (e + 1) * span], TN, preferred_element_type=F32
+            )
+            * root
+        )
+    for e in range(examples):
         even = block[e, pl.ds(0, side, stride=2), :]
         odd = block[e, pl.ds(1, side, stride=2), :]
         half = side // 2
@@ -212,25 +220,35 @@
 
 
 def gram_kernel(
-    n, examples, scale, full_in, rows_in, store_ref, gram_ref, panel, full_ref, rows_ref, sem
+    n, examples, scale, full_in, rows_in, store_ref, gram_ref, panel, full_ref, own_ref, rows_ref, sem
 ):
     me = lax.axis_index("dp")
     j = pl.program_id(0)
     blocks = gram_ref.shape[0] // LANES
     depth = n * 16
     per_tile = 16 // examples
+    tiles = gram_ref.shape[1] // (LANES * per_tile)
+    own = me * blocks // per_tile
+    parts = full_in.shape[1] // tiles
+
+    def part(i):
+        cols = pl.ds(i * tiles, tiles)
+        return pltpu.make_async_copy(full_in.at[:, cols], full_ref.at[:, cols], sem.at[2 + i])
 
     @pl.when(j == 0)
     def _():
-        fetch = pltpu.make_async_copy(full_in, full_ref, sem.at[0])
-        fetch.start()
+        source = full_in.at[:, pl.ds(own, 1)]
+        first = pltpu.make_async_copy(source, own_ref, sem.at[0])
+        first.start()
+        for i in range(parts):
+            part(i).start()
         pltpu.make_async_copy(rows_in, rows_ref, sem.at[1]).start()
-        fetch.wait()
+        first.wait()
         lane = lax.broadcasted_iota(jnp.int32, (LANES, LANES), 1)
         for t in range(blocks):
             block = me * blocks + t
             place = t % per_tile if blocks % per_tile == 0 else block % per_tile
-            columns = full_ref[:, block // per_tile].reshape(depth, LANES).astype(F32)
+            columns = own_ref[:, t // per_tile].reshape(depth, LANES).astype(F32)
             for q in range(depth // LANES):
                 turned = columns[q * LANES : (q + 1) * LANES].T * scale
                 for m in range(per_tile):
@@ -250,7 +268,7 @@
         for r in range(store_ref.shape[1] // LANES):
             store_ref[:, r * LANES : (r + 1) * LANES] = rows_ref[r * 8 : r * 8 + height, :]
 
-    tiles = gram_ref.shape[1] // (LANES * per_tile)
+    part(j).wait()
     right = jnp.concatenate(
         [full_ref[:, j * tiles + t].reshape(depth, LANES) for t in range(tiles)], axis=1
     )
@@ -354,8 +372,9 @@
         scratch_shapes=[
             pltpu.VMEM((16 // examples, panel_width, n * 16), BF16),
             pltpu.VMEM(full.shape, BF16),
+            pltpu.VMEM((n, 1, 16, LANES), BF16),
             pltpu.VMEM(rows.shape, F32),
-            dma((2,)),
+            dma((2 + grid,)),
         ],
         compiler_params=pltpu.CompilerParams(vmem_limit_bytes=60 * 2**20),
         name="gram",

time: 34.5 us -> 33.4 us (0.968)
  Pallas kernels: 33.7 us -> 32.6 us
    pallas_call x1, Pallas kernels: 24.3 us -> 23.5 us  [shards(): pl.pallas_call(functools.partial(features_kernel, n), out_shape=(jax.Shap...]
where the time goes in v3:
time: 33.4 us; the launch traced here: 33.3 us
  Pallas kernels  32.6 us (98%)
  between operations  0.64 us (2%)
    pallas_call x1, Pallas kernels, shards(): pl.pallas_call(functools.partial(features_kernel, n), out_shape=(jax.Shap...  23.5 us
    pallas_call x1, Pallas kernels, shards(): pl.pallas_call(functools.partial(gram_kernel, n, examples, scale), out_sh...  9.1 us

profile of v3, /device:TPU:0, one launch (start us, length us, event | category | flops | bytes accessed | tf_op | source)
XLA Modules:
  0.0 33.3 jit_solution(8335907253993488630)
XLA Ops:
  0.6 23.5 %features.1 = (bf16[16,16,16,128]{3,2,1,0:T(8,128)(2,1)}, f32[512,128]{1,0:T(8,128)}) custom-call(s32[4]{0:T(128)} %lengths_in.1, s32[4]{0:T(128)} %handover_in.1, bf16[704,4096]{1,0:T(8,128)(2,1)} %bitcast.5, bf16[704,1024]{1,0:T(8,128)(2,1)} %bitcast.6, bf16[64,4096]{1,0:T(8,128)(2,1)} %down_ref.1, bf16[64,1024]{1,0:T(8,128)(2,1)} %bitcast.8, ...), custom_call_target="tpu_custom_call" | custom-call | tf_op jit(solution)/shard_map/features/pallas_call | solution.py:303
  24.2 9.1 %gram.1 = (f32[6,8192]{1,0:T(8,128)}, f32[512,8192]{1,0:T(8,128)}) custom-call(bf16[16,16,16,128]{3,2,1,0:T(8,128)(2,1)} %get-tuple-element.4.full_in, f32[512,128]{1,0:T(8,128)} %get-tuple-element.5.rows_in), custom_call_target="tpu_custom_call" | custom-call | tf_op jit(solution)/shard_map/gram/pallas_call | solution.py:360
